TPU v7x, 512 devices: a whole 4x4x16 slice. The times are simulated.
512 devices in a mesh: dp: 32 (over z, core), crow: 4 (over x), ccol: 4 (over y).
Axes of the slice: x: 4, y: 4, z: 16, core: 2. Of those that a mesh axis runs over, the one named last changes fastest.
Arguments:
- data: float32 [16, 262144], P(None, ('dp', 'crow')), may hold values from 0 to 1
- centres: float32 [16, 3072], P(None, 'ccol'), may hold values from 0 to 1
- scales: float32 [16], replicated, may hold values from 0.5 to 1.2
- factor: float32 [3072, 3072], P('crow', 'ccol'), may hold values from -1 to 1, as said below
- block_inv: float32 [12, 256, 256], P('crow'), may hold values from -1 to 2
- iterate: float32 [8, 3072], replicated, may hold values from -6 to 6
- residual: float32 [8, 3072], replicated, may hold values from -6 to 6
- direction: float32 [8, 3072], replicated, may hold values from -6 to 6
Outputs:
- new_iterate: float32 [8, 3072], replicated
- new_residual: float32 [8, 3072], replicated
- new_direction: float32 [8, 3072], replicated
Inputs may be any that keep to these rules, and one draw needn't show every extreme that they name: `factor`: blocks of 256 x 256 on and above the block diagonal are zero.
All inputs are finite; a program needn't handle non-finite values.
Results may differ from a plain program's by a relative error of at most 0.0001.
Values sent between devices are 32-bit elements; how exact they have to be, the bound alone decides.
A program may use at most 64 MiB of HBM per device.

v0:
```python
import jax
import jax.numpy as jnp
from jax import lax
from jax.sharding import PartitionSpec as P

RBLK = 1024
ridge_weight = 0.2
highest = lax.Precision.HIGHEST


def kernel_tile(sample, centre_set, scales):
    scaled_sample = sample / scales[:, None]
    scaled_centres = centre_set / scales[:, None]
    cross_terms = lax.dot_general(
        scaled_centres,
        scaled_sample,
        (((0,), (0,)), ((), ())),
        precision=highest,
        preferred_element_type=jnp.float32,
    )
    distance = (
        jnp.sum(scaled_centres * scaled_centres, axis=0)[:, None]
        + jnp.sum(scaled_sample * scaled_sample, axis=0)[None, :]
        - 2.0 * cross_terms
    )
    return jnp.exp(-0.5 * distance)


def project(weights, tile):
    return jnp.dot(weights, tile, precision=highest, preferred_element_type=jnp.float32)


def pullback(images, tile):
    return lax.dot_general(
        images,
        tile,
        (((1,), (1,)), ((), ())),
        precision=highest,
        preferred_element_type=jnp.float32,
    )


def per_device(data, centres, scales, factor, block_inv, iterate, residual, direction):
    order = block_inv.shape[1]
    local_rows = factor.shape[0]
    local_cols = factor.shape[1]
    per_row = local_rows // order
    per_col = local_cols // order
    nblocks = per_row * lax.axis_size("crow")
    row_place = lax.axis_index("crow")
    col_place = lax.axis_index("ccol")
    solved = jnp.zeros_like(direction)
    for number in reversed(range(nblocks)):
        start = number * order
        owner = number // per_col
        offset = number % per_col * order
        held = number % per_row
        segment = lax.dynamic_slice_in_dim(solved, row_place * local_rows, local_rows, 1)
        partial_value = project(segment, factor[:, offset : offset + order])
        partial_value = jnp.where(col_place == owner, partial_value, 0.0)
        partial_value = lax.psum(partial_value, ("crow", "ccol"))
        piece = project(direction[:, start : start + order] - partial_value, block_inv[held])
        solved = solved.at[:, start : start + order].set(piece)
    own_part = lax.dynamic_slice_in_dim(solved, row_place * local_rows, local_rows, 1)
    solved = lax.all_gather(own_part, "crow", axis=1, tiled=True)
    rows_here = data.shape[1]
    span = min(RBLK, rows_here)
    blocks = rows_here // span
    stacked = data.reshape(data.shape[0], blocks, span).transpose(1, 0, 2)
    width = centres.shape[1]
    mine = lax.dynamic_slice_in_dim(solved, col_place * width, width, 1)

    def forward_images(carry, sample):
        return (carry, project(mine, kernel_tile(sample, centres, scales)))

    _, images = lax.scan(forward_images, jnp.zeros((), jnp.float32), stacked)
    images = lax.psum(images, "ccol")

    def backward_images(total, pair):
        sample, image_rows = pair
        return (total + pullback(image_rows, kernel_tile(sample, centres, scales)), None)

    summed, _ = lax.scan(
        backward_images, jnp.zeros((solved.shape[0], width), jnp.float32), (stacked, images)
    )
    summed = lax.psum(summed, ("dp", "crow"))
    summed = lax.all_gather(summed, "ccol", axis=1, tiled=True)
    total_rows = rows_here * lax.axis_size("dp") * lax.axis_size("crow")
    normal_image = summed / total_rows + ridge_weight * solved
    image = jnp.zeros_like(direction)
    for number in range(nblocks):
        start = number * order
        owner = number // per_row
        held = number % per_row
        offset = held * order
        segment = lax.dynamic_slice_in_dim(image, col_place * local_cols, local_cols, 1)
        leading = jnp.where(col_place == 0, normal_image[:, start : start + order], 0.0)
        term = pullback(
            leading - pullback(segment, factor[offset : offset + order, :]), block_inv[held]
        )
        term = jnp.where(row_place == owner, term, 0.0)
        piece = lax.psum(term, ("crow", "ccol"))
        image = image.at[:, start : start + order].set(piece)
    gamma = jnp.sum(residual * residual, axis=1)
    curvature = jnp.sum(direction * image, axis=1)
    alpha = (gamma / curvature)[:, None]
    new_iterate = iterate + alpha * direction
    new_residual = residual - alpha * image
    gamma_next = jnp.sum(new_residual * new_residual, axis=1)
    new_direction = new_residual + (gamma_next / gamma)[:, None] * direction
    return (new_iterate, new_residual, new_direction)


def solution(mesh):
    placed = (
        P(None, ("dp", "crow")),
        P(None, "ccol"),
        P(),
        P("crow", "ccol"),
        P("crow", None, None),
        P(),
        P(),
        P(),
    )
    return jax.shard_map(
        per_device, mesh=mesh, in_specs=placed, out_specs=(P(), P(), P()), check_vma=False
    )
```

profile of v0, /device:TPU:8, one launch (start us, length us, event | category | flops | bytes accessed | tf_op | source)
XLA Modules:
  0.0 1564.1 jit_solution(2935731484131593567)
XLA Ops:
  16.1 41.8 %psum.182 = f32[8,256]{1,0:T(8,128)S(1)} all-reduce(f32[8,256]{1,0:T(8,128)S(1)} %convolution_select_fusion.34), channel_id=1, replica_groups=mesh['dp'=32,'crow'=4,'ccol'=4] {'crow','ccol'}, use_global_device_ids=true, to_apply=%region_2.3 | all-reduce | flops 2048 | bytes 16384 | tf_op jit(solution)/shard_map/psum | solution.py:61
  60.6 36.0 %psum.183 = f32[8,256]{1,0:T(8,128)S(1)} all-reduce(f32[8,256]{1,0:T(8,128)S(1)} %convolution_select_fusion.33), channel_id=1, replica_groups=mesh['dp'=32,'crow'=4,'ccol'=4] {'crow','ccol'}, use_global_device_ids=true, to_apply=%region_4.5 | all-reduce | flops 2048 | bytes 16384 | tf_op jit(solution)/shard_map/psum | solution.py:61
  98.9 38.1 %psum.184 = f32[8,256]{1,0:T(8,128)S(1)} all-reduce(f32[8,256]{1,0:T(8,128)S(1)} %convolution_select_fusion.31), channel_id=1, replica_groups=mesh['dp'=32,'crow'=4,'ccol'=4] {'crow','ccol'}, use_global_device_ids=true, to_apply=%region_6.7 | all-reduce | flops 2048 | bytes 16384 | tf_op jit(solution)/shard_map/psum | solution.py:61
  176.1 38.2 %psum.186 = f32[8,256]{1,0:T(8,128)S(1)} all-reduce(f32[8,256]{1,0:T(8,128)S(1)} %convolution_select_fusion.27), channel_id=1, replica_groups=mesh['dp'=32,'crow'=4,'ccol'=4] {'crow','ccol'}, use_global_device_ids=true, to_apply=%region_10.11 | all-reduce | flops 2048 | bytes 16384 | tf_op jit(solution)/shard_map/psum | solution.py:61
  252.7 38.0 %psum.188 = f32[8,256]{1,0:T(8,128)S(1)} all-reduce(f32[8,256]{1,0:T(8,128)S(1)} %convolution_select_fusion.23), channel_id=1, replica_groups=mesh['dp'=32,'crow'=4,'ccol'=4] {'crow','ccol'}, use_global_device_ids=true, to_apply=%region_14.15 | all-reduce | flops 2048 | bytes 16384 | tf_op jit(solution)/shard_map/psum | solution.py:61
  291.9 36.0 %psum.189 = f32[8,256]{1,0:T(8,128)S(1)} all-reduce(f32[8,256]{1,0:T(8,128)S(1)} %convolution_select_fusion.21), channel_id=1, replica_groups=mesh['dp'=32,'crow'=4,'ccol'=4] {'crow','ccol'}, use_global_device_ids=true, to_apply=%region_16.17 | all-reduce | flops 2048 | bytes 16384 | tf_op jit(solution)/shard_map/psum | solution.py:61
  329.2 38.0 %psum.190 = f32[8,256]{1,0:T(8,128)S(1)} all-reduce(f32[8,256]{1,0:T(8,128)S(1)} %convolution_select_fusion.19), channel_id=1, replica_groups=mesh['dp'=32,'crow'=4,'ccol'=4] {'crow','ccol'}, use_global_device_ids=true, to_apply=%region_18.19 | all-reduce | flops 2048 | bytes 16384 | tf_op jit(solution)/shard_map/psum | solution.py:61
  368.4 36.0 %psum.191 = f32[8,256]{1,0:T(8,128)S(1)} all-reduce(f32[8,256]{1,0:T(8,128)S(1)} %convolution_select_fusion.17), channel_id=1, replica_groups=mesh['dp'=32,'crow'=4,'ccol'=4] {'crow','ccol'}, use_global_device_ids=true, to_apply=%region_20.21 | all-reduce | flops 2048 | bytes 16384 | tf_op jit(solution)/shard_map/psum | solution.py:61
  405.6 38.0 %psum.192 = f32[8,256]{1,0:T(8,128)S(1)} all-reduce(f32[8,256]{1,0:T(8,128)S(1)} %convolution_select_fusion.15), channel_id=1, replica_groups=mesh['dp'=32,'crow'=4,'ccol'=4] {'crow','ccol'}, use_global_device_ids=true, to_apply=%region_22.23 | all-reduce | flops 2048 | bytes 16384 | tf_op jit(solution)/shard_map/psum | solution.py:61
  444.9 36.0 %psum.193 = f32[8,256]{1,0:T(8,128)S(1)} all-reduce(f32[8,256]{1,0:T(8,128)S(1)} %convolution_select_fusion.13), channel_id=1, replica_groups=mesh['dp'=32,'crow'=4,'ccol'=4] {'crow','ccol'}, use_global_device_ids=true, to_apply=%region_23.24 | all-reduce | flops 2048 | bytes 16384 | tf_op jit(solution)/shard_map/psum | solution.py:61
  508.7 55.2 %all-reduce.4.cloned.1.call-done = f32[2,8,1024]{2,1,0:T(8,128)} async-done(((f32[2,8,1024]{2,1,0:T(8,128)}), f32[2,8,1024]{2,1,0:T(8,128)}) %all-reduce.4.cloned.1.call-update) | async-done | bytes 65552 | tf_op jit(solution)/shard_map/psum | solution.py:77
  584.3 494.7 %psum.195 = f32[8,768]{1,0:T(8,128)S(1)} all-reduce(f32[8,768]{1,0:T(8,128)} %get-tuple-element.356), channel_id=1, replica_groups=mesh['dp'=32,'crow'=4,'ccol'=4] {'dp','crow'}, use_global_device_ids=true, to_apply=%region_33.34 | all-reduce | flops 6144 | bytes 49152 | tf_op jit(solution)/shard_map/psum | solution.py:86
  1091.8 37.8 %psum.196 = f32[8,256]{1,0:T(8,128)S(1)} all-reduce(f32[8,256]{1,0:T(8,128)S(1)} %convolution_select_fusion.11), channel_id=1, replica_groups=mesh['dp'=32,'crow'=4,'ccol'=4] {'crow','ccol'}, use_global_device_ids=true, to_apply=%region_34.35 | all-reduce | flops 2048 | bytes 16384 | tf_op jit(solution)/shard_map/psum | solution.py:102
  1131.2 36.5 %psum.197 = f32[8,256]{1,0:T(8,128)S(1)} all-reduce(f32[8,256]{1,0:T(8,128)S(1)} %convolution_select_fusion.10), channel_id=1, replica_groups=mesh['dp'=32,'crow'=4,'ccol'=4] {'crow','ccol'}, use_global_device_ids=true, to_apply=%region_35.36 | all-reduce | flops 2048 | bytes 16384 | tf_op jit(solution)/shard_map/psum | solution.py:102
  1169.3 37.6 %psum.198 = f32[8,256]{1,0:T(8,128)S(1)} all-reduce(f32[8,256]{1,0:T(8,128)S(1)} %convolution_select_fusion.9), channel_id=1, replica_groups=mesh['dp'=32,'crow'=4,'ccol'=4] {'crow','ccol'}, use_global_device_ids=true, to_apply=%region_36.37 | all-reduce | flops 2048 | bytes 16384 | tf_op jit(solution)/shard_map/psum | solution.py:102
  1208.4 36.6 %psum.199 = f32[8,256]{1,0:T(8,128)S(1)} all-reduce(f32[8,256]{1,0:T(8,128)S(1)} %convolution_select_fusion.8), channel_id=1, replica_groups=mesh['dp'=32,'crow'=4,'ccol'=4] {'crow','ccol'}, use_global_device_ids=true, to_apply=%region_37.38 | all-reduce | flops 2048 | bytes 16384 | tf_op jit(solution)/shard_map/psum | solution.py:102
  1246.7 37.5 %psum.200 = f32[8,256]{1,0:T(8,128)S(1)} all-reduce(f32[8,256]{1,0:T(8,128)S(1)} %convolution_select_fusion.7), channel_id=1, replica_groups=mesh['dp'=32,'crow'=4,'ccol'=4] {'crow','ccol'}, use_global_device_ids=true, to_apply=%region_38.39 | all-reduce | flops 2048 | bytes 16384 | tf_op jit(solution)/shard_map/psum | solution.py:102
  1285.8 36.5 %psum.201 = f32[8,256]{1,0:T(8,128)S(1)} all-reduce(f32[8,256]{1,0:T(8,128)S(1)} %convolution_select_fusion.6), channel_id=1, replica_groups=mesh['dp'=32,'crow'=4,'ccol'=4] {'crow','ccol'}, use_global_device_ids=true, to_apply=%region_39.40 | all-reduce | flops 2048 | bytes 16384 | tf_op jit(solution)/shard_map/psum | solution.py:102
  1324.0 37.5 %psum.202 = f32[8,256]{1,0:T(8,128)S(1)} all-reduce(f32[8,256]{1,0:T(8,128)S(1)} %convolution_select_fusion.5), channel_id=1, replica_groups=mesh['dp'=32,'crow'=4,'ccol'=4] {'crow','ccol'}, use_global_device_ids=true, to_apply=%region_40.41 | all-reduce | flops 2048 | bytes 16384 | tf_op jit(solution)/shard_map/psum | solution.py:102
  1363.1 36.5 %psum.203 = f32[8,256]{1,0:T(8,128)S(1)} all-reduce(f32[8,256]{1,0:T(8,128)S(1)} %convolution_select_fusion.4), channel_id=1, replica_groups=mesh['dp'=32,'crow'=4,'ccol'=4] {'crow','ccol'}, use_global_device_ids=true, to_apply=%region_41.42 | all-reduce | flops 2048 | bytes 16384 | tf_op jit(solution)/shard_map/psum | solution.py:102
  1401.3 37.6 %psum.204 = f32[8,256]{1,0:T(8,128)S(1)} all-reduce(f32[8,256]{1,0:T(8,128)S(1)} %convolution_select_fusion.3), channel_id=1, replica_groups=mesh['dp'=32,'crow'=4,'ccol'=4] {'crow','ccol'}, use_global_device_ids=true, to_apply=%region_42.43 | all-reduce | flops 2048 | bytes 16384 | tf_op jit(solution)/shard_map/psum | solution.py:102
  1440.5 36.5 %psum.205 = f32[8,256]{1,0:T(8,128)S(1)} all-reduce(f32[8,256]{1,0:T(8,128)S(1)} %convolution_select_fusion.2), channel_id=1, replica_groups=mesh['dp'=32,'crow'=4,'ccol'=4] {'crow','ccol'}, use_global_device_ids=true, to_apply=%region_43.44 | all-reduce | flops 2048 | bytes 16384 | tf_op jit(solution)/shard_map/psum | solution.py:102
  1478.6 37.5 %psum.206 = f32[8,256]{1,0:T(8,128)S(1)} all-reduce(f32[8,256]{1,0:T(8,128)S(1)} %convolution_select_fusion.1), channel_id=1, replica_groups=mesh['dp'=32,'crow'=4,'ccol'=4] {'crow','ccol'}, use_global_device_ids=true, to_apply=%region_44.45 | all-reduce | flops 2048 | bytes 16384 | tf_op jit(solution)/shard_map/psum | solution.py:102
  1517.8 36.5 %psum.207 = f32[8,256]{1,0:T(8,128)S(1)} all-reduce(f32[8,256]{1,0:T(8,128)S(1)} %convolution_select_fusion), channel_id=1, replica_groups=mesh['dp'=32,'crow'=4,'ccol'=4] {'crow','ccol'}, use_global_device_ids=true, to_apply=%region_45.46 | all-reduce | flops 2048 | bytes 16384 | tf_op jit(solution)/shard_map/psum | solution.py:102
  (124 shorter events, 211.6 us)
Async XLA Ops:
  7.2 91.3 %copy-start = (f32[768,768]{1,0:T(8,128)S(1)}, f32[768,768]{1,0:T(8,128)}, u32[]{:S(2)}) copy-start(f32[768,768]{1,0:T(8,128)} %param.63) | copy-start | bytes 7077892
  7.2 129.8 %copy-start.1 = (f32[3,256,256]{2,1,0:T(8,128)S(1)}, f32[3,256,256]{2,1,0:T(8,128)}, u32[]{:S(2)}) copy-start(f32[3,256,256]{2,1,0:T(8,128)} %param.64) | copy-start | bytes 2359300
  7.2 167.6 %copy-start.3 = (f32[8,3072]{1,0:T(8,128)S(1)}, f32[8,3072]{1,0:T(8,128)}, u32[]{:S(2)}) copy-start(f32[8,3072]{1,0:T(8,128)} %param.67) | copy-start | bytes 294916
  7.2 556.7 %all-reduce.4.cloned.1.call-start = ((), (), s32[]{:S(2)}) async-start(), calls=%async_computation | async-start | bytes 131072 | tf_op jit(solution)/shard_map/psum | solution.py:77
  328.7 165.1 %copy-start.6 = (f32[16,2048]{1,0:T(8,128)S(1)}, f32[16,2048]{1,0:T(8,128)}, u32[]{:S(2)}) copy-start(f32[16,2048]{1,0:T(8,128)} %param.60) | copy-start | bytes 393220
  329.2 166.4 %copy-start.2 = (f32[16,768]{1,0:T(8,128)S(1)}, f32[16,768]{1,0:T(8,128)}, u32[]{:S(2)}) copy-start(f32[16,768]{1,0:T(8,128)} %param.61) | copy-start | bytes 147460
  329.2 166.4 %copy-start.4 = (f32[16]{0:T(128)S(1)}, f32[16]{0:T(128)}, u32[]{:S(2)}) copy-start(f32[16]{0:T(128)} %param.62) | copy-start | bytes 196
  1555.5 1.7 copy-start.5
Sparse Core Ops, SparseCore 0:
  507.7 56.0 all-reduce.3
where the time goes:
time: 1570 us; the launch traced here: 1560 us
  blocking collectives  1410 us (90%)
  matrix products  62.8 us (4%)
  waiting for transfers between devices  55.2 us (4%)
  other arithmetic  18.8 us (1%)
    psum x1, blocking collectives, per_device(): summed = lax.psum(summed, ('dp', 'crow'))  495 us
    psum x12, blocking collectives, per_device(): partial_value = lax.psum(partial_value, ('crow', 'ccol'))  448 us
    psum x12, blocking collectives, per_device(): piece = lax.psum(term, ('crow', 'ccol'))  445 us
    psum x1, waiting for transfers between devices, per_device(): images = lax.psum(images, 'ccol')  55.2 us
  transfers between devices with their start and end apart: 1, of which 1 were waited for; matrix products, arithmetic and copies ran while one was open for 0% of the time, Pallas kernels for 0%

commit v1 on v0

--- a/solution.py
+++ b/solution.py
@@ -74,7 +74,9 @@
         return (carry, project(mine, kernel_tile(sample, centres, scales)))
 
     _, images = lax.scan(forward_images, jnp.zeros((), jnp.float32), stacked)
-    images = lax.psum(images, "ccol")
+    images = images
+    for hop in (1, 2):
+        images = images + lax.ppermute(images, "ccol", [(dev, dev ^ hop) for dev in range(4)])
 
     def backward_images(total, pair):
         sample, image_rows = pair

time: 1570 us -> 1510 us (0.962)
  waiting for transfers between devices: 55.2 us -> 7.23 us
    psum x1 -> x0, waiting for transfers between devices: 55.2 us -> none  [per_device(): images = lax.psum(images, 'ccol')]
  transfers between devices with their start and end apart: 1 -> 2, of which waited for: 1 -> 2; matrix products, arithmetic and copies ran while one was open for 0% -> 0% of each run, Pallas kernels for 0% -> 0%
where the time goes in v1:
time: 1510 us
  blocking collectives  1410 us (93%)
  matrix products  62.8 us (4%)
  other arithmetic  20.2 us (1%)
    psum x1, blocking collectives, per_device(): summed = lax.psum(summed, ('dp', 'crow'))  493 us
    psum x12, blocking collectives, per_device(): partial_value = lax.psum(partial_value, ('crow', 'ccol'))  448 us
    psum x12, blocking collectives, per_device(): piece = lax.psum(term, ('crow', 'ccol'))  444 us
  transfers between devices with their start and end apart: 2, of which 2 were waited for; matrix products, arithmetic and copies ran while one was open for 0% of the time, Pallas kernels for 0%

profile of v1, /device:TPU:8, one launch (start us, length us, event | category | flops | bytes accessed | tf_op | source)
XLA Modules:
  0.0 1506.9 jit_solution(4306174650583470350)
XLA Ops:
  9.4 41.8 %psum.175 = f32[8,256]{1,0:T(8,128)S(1)} all-reduce(f32[8,256]{1,0:T(8,128)S(1)} %convolution_select_fusion.34), channel_id=1, replica_groups=mesh['dp'=32,'crow'=4,'ccol'=4] {'crow','ccol'}, use_global_device_ids=true, to_apply=%region_2.3 | all-reduce | flops 2048 | bytes 16384 | tf_op jit(solution)/shard_map/psum | solution.py:61
  54.0 36.0 %psum.176 = f32[8,256]{1,0:T(8,128)S(1)} all-reduce(f32[8,256]{1,0:T(8,128)S(1)} %convolution_select_fusion.33), channel_id=1, replica_groups=mesh['dp'=32,'crow'=4,'ccol'=4] {'crow','ccol'}, use_global_device_ids=true, to_apply=%region_4.5 | all-reduce | flops 2048 | bytes 16384 | tf_op jit(solution)/shard_map/psum | solution.py:61
  92.2 38.1 %psum.177 = f32[8,256]{1,0:T(8,128)S(1)} all-reduce(f32[8,256]{1,0:T(8,128)S(1)} %convolution_select_fusion.31), channel_id=1, replica_groups=mesh['dp'=32,'crow'=4,'ccol'=4] {'crow','ccol'}, use_global_device_ids=true, to_apply=%region_6.7 | all-reduce | flops 2048 | bytes 16384 | tf_op jit(solution)/shard_map/psum | solution.py:61
  169.4 38.1 %psum.179 = f32[8,256]{1,0:T(8,128)S(1)} all-reduce(f32[8,256]{1,0:T(8,128)S(1)} %convolution_select_fusion.27), channel_id=1, replica_groups=mesh['dp'=32,'crow'=4,'ccol'=4] {'crow','ccol'}, use_global_device_ids=true, to_apply=%region_10.11 | all-reduce | flops 2048 | bytes 16384 | tf_op jit(solution)/shard_map/psum | solution.py:61
  208.8 36.0 %psum.180 = f32[8,256]{1,0:T(8,128)S(1)} all-reduce(f32[8,256]{1,0:T(8,128)S(1)} %convolution_select_fusion.25), channel_id=1, replica_groups=mesh['dp'=32,'crow'=4,'ccol'=4] {'crow','ccol'}, use_global_device_ids=true, to_apply=%region_12.13 | all-reduce | flops 2048 | bytes 16384 | tf_op jit(solution)/shard_map/psum | solution.py:61
  246.1 38.0 %psum.181 = f32[8,256]{1,0:T(8,128)S(1)} all-reduce(f32[8,256]{1,0:T(8,128)S(1)} %convolution_select_fusion.23), channel_id=1, replica_groups=mesh['dp'=32,'crow'=4,'ccol'=4] {'crow','ccol'}, use_global_device_ids=true, to_apply=%region_14.15 | all-reduce | flops 2048 | bytes 16384 | tf_op jit(solution)/shard_map/psum | solution.py:61
  285.2 36.0 %psum.182 = f32[8,256]{1,0:T(8,128)S(1)} all-reduce(f32[8,256]{1,0:T(8,128)S(1)} %convolution_select_fusion.21), channel_id=1, replica_groups=mesh['dp'=32,'crow'=4,'ccol'=4] {'crow','ccol'}, use_global_device_ids=true, to_apply=%region_16.17 | all-reduce | flops 2048 | bytes 16384 | tf_op jit(solution)/shard_map/psum | solution.py:61
  322.5 38.0 %psum.183 = f32[8,256]{1,0:T(8,128)S(1)} all-reduce(f32[8,256]{1,0:T(8,128)S(1)} %convolution_select_fusion.19), channel_id=1, replica_groups=mesh['dp'=32,'crow'=4,'ccol'=4] {'crow','ccol'}, use_global_device_ids=true, to_apply=%region_18.19 | all-reduce | flops 2048 | bytes 16384 | tf_op jit(solution)/shard_map/psum | solution.py:61
  361.8 36.0 %psum.184 = f32[8,256]{1,0:T(8,128)S(1)} all-reduce(f32[8,256]{1,0:T(8,128)S(1)} %convolution_select_fusion.17), channel_id=1, replica_groups=mesh['dp'=32,'crow'=4,'ccol'=4] {'crow','ccol'}, use_global_device_ids=true, to_apply=%region_20.21 | all-reduce | flops 2048 | bytes 16384 | tf_op jit(solution)/shard_map/psum | solution.py:61
  399.0 38.0 %psum.185 = f32[8,256]{1,0:T(8,128)S(1)} all-reduce(f32[8,256]{1,0:T(8,128)S(1)} %convolution_select_fusion.15), channel_id=1, replica_groups=mesh['dp'=32,'crow'=4,'ccol'=4] {'crow','ccol'}, use_global_device_ids=true, to_apply=%region_22.23 | all-reduce | flops 2048 | bytes 16384 | tf_op jit(solution)/shard_map/psum | solution.py:61
  438.2 36.0 %psum.186 = f32[8,256]{1,0:T(8,128)S(1)} all-reduce(f32[8,256]{1,0:T(8,128)S(1)} %convolution_select_fusion.13), channel_id=1, replica_groups=mesh['dp'=32,'crow'=4,'ccol'=4] {'crow','ccol'}, use_global_device_ids=true, to_apply=%region_23.24 | all-reduce | flops 2048 | bytes 16384 | tf_op jit(solution)/shard_map/psum | solution.py:61
  537.0 492.6 %psum.187 = f32[8,768]{1,0:T(8,128)S(1)} all-reduce(f32[8,768]{1,0:T(8,128)} %get-tuple-element.356), channel_id=1, replica_groups=mesh['dp'=32,'crow'=4,'ccol'=4] {'dp','crow'}, use_global_device_ids=true, to_apply=%region_32.33 | all-reduce | flops 6144 | bytes 49152 | tf_op jit(solution)/shard_map/psum | solution.py:88
  1041.6 37.5 %psum.188 = f32[8,256]{1,0:T(8,128)S(1)} all-reduce(f32[8,256]{1,0:T(8,128)S(1)} %convolution_select_fusion.11), channel_id=1, replica_groups=mesh['dp'=32,'crow'=4,'ccol'=4] {'crow','ccol'}, use_global_device_ids=true, to_apply=%region_33.34 | all-reduce | flops 2048 | bytes 16384 | tf_op jit(solution)/shard_map/psum | solution.py:104
  1080.8 36.8 %psum.189 = f32[8,256]{1,0:T(8,128)S(1)} all-reduce(f32[8,256]{1,0:T(8,128)S(1)} %convolution_select_fusion.10), channel_id=1, replica_groups=mesh['dp'=32,'crow'=4,'ccol'=4] {'crow','ccol'}, use_global_device_ids=true, to_apply=%region_34.35 | all-reduce | flops 2048 | bytes 16384 | tf_op jit(solution)/shard_map/psum | solution.py:104
  1119.1 37.3 %psum.190 = f32[8,256]{1,0:T(8,128)S(1)} all-reduce(f32[8,256]{1,0:T(8,128)S(1)} %convolution_select_fusion.9), channel_id=1, replica_groups=mesh['dp'=32,'crow'=4,'ccol'=4] {'crow','ccol'}, use_global_device_ids=true, to_apply=%region_35.36 | all-reduce | flops 2048 | bytes 16384 | tf_op jit(solution)/shard_map/psum | solution.py:104
  1158.0 36.7 %psum.191 = f32[8,256]{1,0:T(8,128)S(1)} all-reduce(f32[8,256]{1,0:T(8,128)S(1)} %convolution_select_fusion.8), channel_id=1, replica_groups=mesh['dp'=32,'crow'=4,'ccol'=4] {'crow','ccol'}, use_global_device_ids=true, to_apply=%region_36.37 | all-reduce | flops 2048 | bytes 16384 | tf_op jit(solution)/shard_map/psum | solution.py:104
  1196.4 37.4 %psum.192 = f32[8,256]{1,0:T(8,128)S(1)} all-reduce(f32[8,256]{1,0:T(8,128)S(1)} %convolution_select_fusion.7), channel_id=1, replica_groups=mesh['dp'=32,'crow'=4,'ccol'=4] {'crow','ccol'}, use_global_device_ids=true, to_apply=%region_37.38 | all-reduce | flops 2048 | bytes 16384 | tf_op jit(solution)/shard_map/psum | solution.py:104
  1235.5 36.6 %psum.193 = f32[8,256]{1,0:T(8,128)S(1)} all-reduce(f32[8,256]{1,0:T(8,128)S(1)} %convolution_select_fusion.6), channel_id=1, replica_groups=mesh['dp'=32,'crow'=4,'ccol'=4] {'crow','ccol'}, use_global_device_ids=true, to_apply=%region_38.39 | all-reduce | flops 2048 | bytes 16384 | tf_op jit(solution)/shard_map/psum | solution.py:104
  1273.7 37.4 %psum.194 = f32[8,256]{1,0:T(8,128)S(1)} all-reduce(f32[8,256]{1,0:T(8,128)S(1)} %convolution_select_fusion.5), channel_id=1, replica_groups=mesh['dp'=32,'crow'=4,'ccol'=4] {'crow','ccol'}, use_global_device_ids=true, to_apply=%region_39.40 | all-reduce | flops 2048 | bytes 16384 | tf_op jit(solution)/shard_map/psum | solution.py:104
  1312.7 36.6 %psum.195 = f32[8,256]{1,0:T(8,128)S(1)} all-reduce(f32[8,256]{1,0:T(8,128)S(1)} %convolution_select_fusion.4), channel_id=1, replica_groups=mesh['dp'=32,'crow'=4,'ccol'=4] {'crow','ccol'}, use_global_device_ids=true, to_apply=%region_40.41 | all-reduce | flops 2048 | bytes 16384 | tf_op jit(solution)/shard_map/psum | solution.py:104
  1351.0 37.6 %psum.196 = f32[8,256]{1,0:T(8,128)S(1)} all-reduce(f32[8,256]{1,0:T(8,128)S(1)} %convolution_select_fusion.3), channel_id=1, replica_groups=mesh['dp'=32,'crow'=4,'ccol'=4] {'crow','ccol'}, use_global_device_ids=true, to_apply=%region_41.42 | all-reduce | flops 2048 | bytes 16384 | tf_op jit(solution)/shard_map/psum | solution.py:104
  1390.2 36.5 %psum.197 = f32[8,256]{1,0:T(8,128)S(1)} all-reduce(f32[8,256]{1,0:T(8,128)S(1)} %convolution_select_fusion.2), channel_id=1, replica_groups=mesh['dp'=32,'crow'=4,'ccol'=4] {'crow','ccol'}, use_global_device_ids=true, to_apply=%region_42.43 | all-reduce | flops 2048 | bytes 16384 | tf_op jit(solution)/shard_map/psum | solution.py:104
  1428.2 37.6 %psum.198 = f32[8,256]{1,0:T(8,128)S(1)} all-reduce(f32[8,256]{1,0:T(8,128)S(1)} %convolution_select_fusion.1), channel_id=1, replica_groups=mesh['dp'=32,'crow'=4,'ccol'=4] {'crow','ccol'}, use_global_device_ids=true, to_apply=%region_43.44 | all-reduce | flops 2048 | bytes 16384 | tf_op jit(solution)/shard_map/psum | solution.py:104
  1467.5 36.5 %psum.199 = f32[8,256]{1,0:T(8,128)S(1)} all-reduce(f32[8,256]{1,0:T(8,128)S(1)} %convolution_select_fusion), channel_id=1, replica_groups=mesh['dp'=32,'crow'=4,'ccol'=4] {'crow','ccol'}, use_global_device_ids=true, to_apply=%region_44.45 | all-reduce | flops 2048 | bytes 16384 | tf_op jit(solution)/shard_map/psum | solution.py:104
  (127 shorter events, 189.3 us)
Async XLA Ops:
  0.6 91.2 %copy-start = (f32[768,768]{1,0:T(8,128)S(1)}, f32[768,768]{1,0:T(8,128)}, u32[]{:S(2)}) copy-start(f32[768,768]{1,0:T(8,128)} %param.63) | copy-start | bytes 7077892
  0.6 129.7 %copy-start.1 = (f32[3,256,256]{2,1,0:T(8,128)S(1)}, f32[3,256,256]{2,1,0:T(8,128)}, u32[]{:S(2)}) copy-start(f32[3,256,256]{2,1,0:T(8,128)} %param.64) | copy-start | bytes 2359300
  0.7 167.5 %copy-start.3 = (f32[8,3072]{1,0:T(8,128)S(1)}, f32[8,3072]{1,0:T(8,128)}, u32[]{:S(2)}) copy-start(f32[8,3072]{1,0:T(8,128)} %param.67) | copy-start | bytes 294916
  322.1 165.1 %copy-start.6 = (f32[16,2048]{1,0:T(8,128)S(1)}, f32[16,2048]{1,0:T(8,128)}, u32[]{:S(2)}) copy-start(f32[16,2048]{1,0:T(8,128)} %param.60) | copy-start | bytes 393220
  322.5 166.4 %copy-start.2 = (f32[16,768]{1,0:T(8,128)S(1)}, f32[16,768]{1,0:T(8,128)}, u32[]{:S(2)}) copy-start(f32[16,768]{1,0:T(8,128)} %param.61) | copy-start | bytes 147460
  322.5 166.4 %copy-start.4 = (f32[16]{0:T(128)S(1)}, f32[16]{0:T(128)}, u32[]{:S(2)}) copy-start(f32[16]{0:T(128)} %param.62) | copy-start | bytes 196
  501.0 6.5 collective-permute-start
  508.3 7.7 collective-permute-start.1
  1505.2 1.7 copy-start.5
